TPU v7x, 256 devices: a whole 4x4x8 slice. The times are simulated.
256 devices in a mesh: pair: 64 (over x, z, core), fock: 4 (over y).
Axes of the slice: x: 4, y: 4, z: 8, core: 2. Of those that a mesh axis runs over, the one named last changes fastest.
Arguments:
- three_center: bfloat16 [3072, 64, 4096], P('pair', 'fock'), may hold values from -0.75 to 0.75
- coefficients: bfloat16 [32, 19968], replicated, may hold values from -0.23925781 to 0.23925781
- metric_inv: bfloat16 [512, 512], replicated, as said below
- target_owner: int32 [3072, 1], P('pair'), may hold values from 0 to 63; in each aligned block of 48 rows (0 to 47, 48 to 95, ...) at most 2 rows name the same one
- row_slot: int32 [3072], P('pair'), may hold values from 0 to 7
- aux_block: int32 [3072], P('pair'), may hold values from 0 to 7
- ao_block: int32 [3072], P('pair'), may hold values from 0 to 311
Outputs:
- exchange: bfloat16 [32768, 512], P(('pair', 'fock'))
Inputs may be any that keep to these rules, and one draw needn't show every extreme that they name: `target_owner`: among the 48 blocks of one index of pair, no owner is named more than 2 times; some owner is named exactly 2 times. `metric_inv`: symmetric.
All inputs are finite; a program needn't handle non-finite values.
Results may differ from a plain program's by a relative error of at most 0.0033.
Values may be sent and summed in bfloat16 or wider, within the bound.
No kernel may reach another device: no remote copies, remote signals or barrier semaphores. Data moves between devices by JAX's collectives and lax.ppermute only.
A program may use at most 128 MiB of HBM per device.

v0:
```python
import jax
import jax.numpy as jnp
from jax import lax
from jax.sharding import PartitionSpec as P

BLK = 64
AUXB = 8
AOB = 312
ROWB = 8
NAUX = 512


def body(three_center, coefficients, metric_inv, target_owner, row_slot, aux_block, ao_block):
    trip_count = three_center.shape[0]
    rows_mine = three_center.shape[1]
    orbitals = coefficients.shape[0]
    block = BLK
    owners = lax.axis_size("pair")
    capacity = max(2, 2 * trip_count // owners)
    combos = ROWB * AUXB
    width = ROWB * block
    unit_size = rows_mine * orbitals * block
    coef_blocks = coefficients.reshape(orbitals, AOB, block)
    picked = jnp.take(coef_blocks, ao_block, axis=1)
    tensor = three_center.reshape(trip_count, rows_mine, block, block)
    units = jnp.einsum("tmlp,itl->tmip", tensor, picked, preferred_element_type=jnp.float32)
    units = units.astype(jnp.bfloat16).reshape(trip_count, unit_size)
    target = target_owner[:, 0]
    combo = row_slot * AUXB + aux_block
    counter = jnp.arange(trip_count, dtype=jnp.int32)
    earlier = (target[:, None] == target[None, :]) & (counter[None, :] < counter[:, None])
    arrival = jnp.sum(earlier.astype(jnp.int32), axis=1)
    position = target * capacity + arrival
    slots = jnp.arange(owners * capacity, dtype=jnp.int32)
    placing = slots[:, None] == position[None, :]
    outgoing = jnp.dot(placing.astype(jnp.bfloat16), units, preferred_element_type=jnp.float32)
    outgoing = outgoing.astype(jnp.bfloat16).reshape(owners, capacity, unit_size)
    out_tags = jnp.max(jnp.where(placing, combo[None, :], -1), axis=1).reshape(owners, capacity)
    combo_ids = jnp.arange(combos, dtype=jnp.int32)
    incoming, in_tags = (
        lax.all_to_all(outgoing, "pair", split_axis=0, concat_axis=0, tiled=True),
        lax.all_to_all(out_tags, "pair", split_axis=0, concat_axis=0, tiled=True),
    )
    selector = (in_tags.reshape(-1)[None, :] == combo_ids[:, None]).astype(jnp.bfloat16)
    summed = jnp.dot(selector, incoming.reshape(-1, unit_size), preferred_element_type=jnp.float32)
    gathered = summed.astype(jnp.bfloat16).reshape(ROWB, AUXB, rows_mine, orbitals, block)
    gathered = gathered.transpose(0, 2, 3, 1, 4).reshape(ROWB, rows_mine, orbitals, NAUX)
    complete = lax.all_gather(gathered, "fock", axis=1, tiled=True)
    complete = complete.reshape(width, orbitals * NAUX)
    share = width // lax.axis_size("fock")
    mine = lax.dynamic_slice_in_dim(complete, lax.axis_index("fock") * share, share, 0)
    fitted = jnp.dot(mine.reshape(-1, NAUX), metric_inv, preferred_element_type=jnp.float32)
    left = fitted.astype(jnp.bfloat16).reshape(share, orbitals * NAUX)
    return jnp.dot(left, complete.T, preferred_element_type=jnp.float32).astype(jnp.bfloat16)


def solution(mesh):
    in_specs = (P("pair", "fock", None), P(), P(), P("pair", None), P("pair"), P("pair"), P("pair"))
    out_specs = P(("pair", "fock"), None)
    return jax.shard_map(body, mesh=mesh, in_specs=in_specs, out_specs=out_specs, check_vma=False)
```

profile of v0, /device:TPU:1, one launch (start us, length us, event | category | flops | bytes accessed | tf_op | source)
XLA Modules:
  0.0 561.6 jit_solution(9736071142861097293)
XLA Ops:
  6.5 0.9 convert_reduce_fusion
  7.4 0.7 multiply_add_fusion
  8.2 0.8 all_to_all.9
  9.0 13.0 %all-to-all-start = ((s32[64,1,2]{2,1,0:T(1,128)}), s32[64,1,2]{2,1,0:T(1,128)S(1)}, u32[]{:S(2)}, u32[]{:S(2)}) async-start(s32[64,1,2]{2,1,0:T(1,128)} %bitcast.1), calls=%async_computation | async-start | bytes 65536 | tf_op jit(solution)/shard_map/all_to_all | solution.py:42
  22.0 0.7 compare_select_fusion
  22.7 0.7 compare_and_fusion
  23.3 17.9 %reshape.52 = bf16[48,16,64,64]{3,2,1,0:T(8,128)(2,1)} reshape(bf16[48,16,4096]{2,1,0:T(8,128)(2,1)} %param.7) | data formatting | bytes 12582912 | tf_op jit(solution)/shard_map/reshape | solution.py:25
  41.2 2.6 reshape.51
  43.8 1.9 copy.14
  45.7 2.3 gather_fusion
  48.1 9.0 %convert_bitcast_fusion = bf16[48,16,32,64]{3,2,1,0:T(8,128)(2,1)} fusion(bf16[48,16,64,64]{3,2,1,0:T(8,128)(2,1)} %reshape.52, bf16[48,32,64]{2,1,0:T(8,128)(2,1)S(1)} %gather_fusion, pred[48]{0:T(512)(128)(4,1)S(1)} %compare_and_fusion), kind=kOutput, calls=%fused_computation.4 | convolution fusion | flops 202997760 | bytes 9633840 | tf_op jit(solution)/shard_map/tmlp,itl->tmip/dot_general | solution.py:26
  57.1 8.3 %reshape.53 = bf16[48,32768]{1,0:T(8,128)(2,1)} reshape(bf16[48,16,32,64]{3,2,1,0:T(8,128)(2,1)} %convert_bitcast_fusion) | data formatting | bytes 6291456 | tf_op jit(solution)/shard_map/reshape | solution.py:27
  65.4 7.5 %convolution_convert_fusion = bf16[128,32768]{1,0:T(8,128)(2,1)} fusion(bf16[48,32768]{1,0:T(8,128)(2,1)} %reshape.53, s32[48]{0:T(128)S(1)} %get-tuple-element.6), kind=kOutput, calls=%fused_computation.1 | convolution fusion | flops 406853632 | bytes 11534528 | tf_op jit(solution)/shard_map/dot_general | solution.py:36
  72.9 14.2 %reshape.54 = bf16[64,2,32768]{2,1,0:T(2,128)(2,1)} reshape(bf16[128,32768]{1,0:T(8,128)(2,1)} %convolution_convert_fusion) | data formatting | bytes 16777216 | tf_op jit(solution)/shard_map/reshape | solution.py:37
  87.1 10.5 %all-to-all-start.1 = ((bf16[64,2,32768]{2,1,0:T(2,128)(2,1)}), bf16[64,2,32768]{2,1,0:T(2,128)(2,1)}, u32[]{:S(2)}, u32[]{:S(2)}) async-start(bf16[64,2,32768]{2,1,0:T(2,128)(2,1)} %reshape.54), calls=%async_computation.1 | async-start | bytes 16777216 | tf_op jit(solution)/shard_map/all_to_all | solution.py:41
  97.6 0.2 all-gather.2.cloned.1.call-start
  97.8 0.5 broadcast.26
  98.4 0.7 reduce.3
  99.2 184.2 %all-to-all-done.1 = bf16[64,2,32768]{2,1,0:T(2,128)(2,1)} async-done(((bf16[64,2,32768]{2,1,0:T(2,128)(2,1)}), bf16[64,2,32768]{2,1,0:T(2,128)(2,1)}, u32[]{:S(2)}, u32[]{:S(2)}) %all-to-all-start.1) | async-done | bytes 8388640 | tf_op jit(solution)/shard_map/all_to_all | solution.py:41
  283.4 13.2 %reshape.55 = bf16[128,32768]{1,0:T(8,128)(2,1)} reshape(bf16[64,2,32768]{2,1,0:T(2,128)(2,1)} %all-to-all-done.1) | data formatting | bytes 16777216 | tf_op jit(solution)/shard_map/reshape | solution.py:45
  296.6 6.6 %convolution_convert_fusion.1 = bf16[64,32768]{1,0:T(8,128)(2,1)} fusion(bf16[128,32768]{1,0:T(8,128)(2,1)} %reshape.55, s32[128]{0:T(128)S(1)} %eq.47), kind=kOutput, calls=%fused_computation.2 | convolution fusion | flops 538976256 | bytes 12583424 | tf_op jit(solution)/shard_map/dot_general | solution.py:45
  303.1 11.4 %reshape.56 = bf16[8,8,16,32,64]{4,3,2,1,0:T(8,128)(2,1)} reshape(bf16[64,32768]{1,0:T(8,128)(2,1)} %convolution_convert_fusion.1) | data formatting | bytes 8388608 | tf_op jit(solution)/shard_map/reshape | solution.py:46
  314.5 16.5 %copy.19 = bf16[8,8,16,32,64]{4,1,3,2,0:T(8,128)(2,1)} copy(bf16[8,8,16,32,64]{4,3,2,1,0:T(8,128)(2,1)} %reshape.56) | data formatting | bytes 8388608 | tf_op jit(solution)/shard_map/reshape | solution.py:46
  330.9 11.8 %reshape.57 = bf16[8,16,32,512]{3,2,1,0:T(8,128)(2,1)} reshape(bf16[8,16,32,8,64]{4,3,2,1,0:T(8,128)(2,1)} %bitcast.31) | data formatting | bytes 8388608 | tf_op jit(solution)/shard_map/reshape | solution.py:47
  342.7 153.5 %all-gather.2.cloned.1.call-done = bf16[8,64,32,512]{3,2,1,0:T(8,128)(2,1)} async-done(((bf16[8,16,32,512]{3,2,1,0:T(8,128)(2,1)}), bf16[8,64,32,512]{3,2,1,0:T(8,128)(2,1)}) %all-gather.2.cloned.1.call-update) | async-done | bytes 16777232 | tf_op jit(solution)/shard_map/all_gather | solution.py:48
  496.2 15.8 %copy.17 = bf16[64,8,32,512]{3,1,2,0:T(8,128)(2,1)S(1)} copy(bf16[64,8,32,512]{3,2,1,0:T(8,128)(2,1)} %bitcast.32) | data formatting | bytes 33554432
  512.1 5.7 %copy-done.1 = bf16[64,8,32,512]{3,1,2,0:T(8,128)(2,1)} copy-done((bf16[64,8,32,512]{3,1,2,0:T(8,128)(2,1)}, bf16[64,8,32,512]{3,1,2,0:T(8,128)(2,1)S(1)}, u32[]{:S(2)}) %copy-start.1) | copy-done | bytes 16777240
  517.8 2.3 constant_dynamic-slice_fusion
  520.1 7.4 %reshape.59 = bf16[4096,512]{1,0:T(8,128)(2,1)} reshape(bf16[128,16384]{1,0:T(8,128)(2,1)} %constant_dynamic-slice_fusion) | data formatting | bytes 8388608 | tf_op jit(solution)/shard_map/reshape | solution.py:52
  527.4 6.5 %convolution_convert_fusion.2 = bf16[4096,512]{1,0:T(8,128)(2,1)} fusion(bf16[4096,512]{1,0:T(8,128)(2,1)} %reshape.59, bf16[512,512]{1,0:T(8,128)(2,1)S(1)} %copy-done), kind=kOutput, calls=%fused_computation.5 | convolution fusion | flops 2149580800 | bytes 8912896 | tf_op jit(solution)/shard_map/dot_general | solution.py:52
  533.9 7.4 %reshape.60 = bf16[128,16384]{1,0:T(8,128)(2,1)} reshape(bf16[4096,512]{1,0:T(8,128)(2,1)} %convolution_convert_fusion.2) | data formatting | bytes 8388608 | tf_op jit(solution)/shard_map/reshape | solution.py:53
  541.3 13.4 %convolution_convert_fusion.3 = bf16[128,512]{1,0:T(8,128)(2,1)} fusion(bf16[128,16384]{1,0:T(8,128)(2,1)} %reshape.60, bf16[512,16384]{1,0:T(8,128)(2,1)} %bitcast.30), kind=kOutput, calls=%fused_computation.6 | convolution fusion | flops 2147549184 | bytes 21102592 | tf_op jit(solution)/shard_map/dot_general | solution.py:54
  (8 shorter events, 0.3 us)
Async XLA Ops:
  6.5 520.9 %copy-start = (bf16[512,512]{1,0:T(8,128)(2,1)S(1)}, bf16[512,512]{1,0:T(8,128)(2,1)}, u32[]{:S(2)}) copy-start(bf16[512,512]{1,0:T(8,128)(2,1)} %param.9) | copy-start | bytes 1572868
  9.0 78.1 %all-to-all-start = ((s32[64,1,2]{2,1,0:T(1,128)}), s32[64,1,2]{2,1,0:T(1,128)S(1)}, u32[]{:S(2)}, u32[]{:S(2)}) async-start(s32[64,1,2]{2,1,0:T(1,128)} %bitcast.1), calls=%async_computation | async-start | bytes 65536 | tf_op jit(solution)/shard_map/all_to_all | solution.py:42
  87.1 196.3 %all-to-all-start.1 = ((bf16[64,2,32768]{2,1,0:T(2,128)(2,1)}), bf16[64,2,32768]{2,1,0:T(2,128)(2,1)}, u32[]{:S(2)}, u32[]{:S(2)}) async-start(bf16[64,2,32768]{2,1,0:T(2,128)(2,1)} %reshape.54), calls=%async_computation.1 | async-start | bytes 16777216 | tf_op jit(solution)/shard_map/all_to_all | solution.py:41
  97.6 398.6 %all-gather.2.cloned.1.call-start = ((), (), s32[]{:S(2)}) async-start(), calls=%async_computation.2 | async-start | bytes 20971520 | tf_op jit(solution)/shard_map/all_gather | solution.py:48
  512.1 5.7 %copy-start.1 = (bf16[64,8,32,512]{3,1,2,0:T(8,128)(2,1)}, bf16[64,8,32,512]{3,1,2,0:T(8,128)(2,1)S(1)}, u32[]{:S(2)}) copy-start(bf16[64,8,32,512]{3,1,2,0:T(8,128)(2,1)S(1)} %copy.17) | copy-start | bytes 50331652
Sparse Core Ops, SparseCore 0:
  342.9 153.3 all-gather.1
where the time goes:
time: 564 us; the launch traced here: 562 us
  waiting for transfers between devices  338 us (60%)
  local copies, waits for them, and re-layouts  140 us (25%)
  matrix products  43 us (8%)
  starting transfers between devices  23.7 us (4%)
  between operations  13.5 us (2%)
    all_to_all x1, waiting for transfers between devices, body(): lax.all_to_all(outgoing, 'pair', split_axis=0, concat_axis=0, tiled=True)  184 us
    all_gather x1, waiting for transfers between devices, body(): complete = lax.all_gather(gathered, 'fock', axis=1, tiled=True)  153 us
    reshape x2, local copies, waits for them, and re-layouts, body(): summed.astype(jnp.bfloat16).reshape(ROWB, AUXB, rows_mine, orbitals, block)  27.8 us
    unnamed x5, local copies, waits for them, and re-layouts  21.6 us
    reshape x1, local copies, waits for them, and re-layouts, body(): tensor = three_center.reshape(trip_count, rows_mine, block, block)  17.9 us
    reshape x1, local copies, waits for them, and re-layouts, body(): outgoing.astype(jnp.bfloat16).reshape(owners, capacity, unit_size)  14.2 us
    dot_general x1, matrix products, body(): jnp.dot(left, complete.T, preferred_element_type=jnp.float32)  13.4 us
    reshape x1, local copies, waits for them, and re-layouts, body(): incoming.reshape(-1, unit_size)  13.2 us
  transfers between devices with their start and end apart: 3, of which 2 were waited for; matrix products, arithmetic and copies ran while one was open for 12% of the time, Pallas kernels for 0%

commit v1 on v0

v1 whole, which is shorter than its diff:
```python
import functools

import jax
import jax.numpy as jnp
from jax import lax
from jax.experimental import pallas as pl
from jax.experimental.pallas import tpu as pltpu
from jax.sharding import Mesh, PartitionSpec as P

BLK = 64
AUXB = 8
ROWB = 8
NAUX = 512
LANES = 128
SLOTS = 4
AXES = ("x", "z", "c", "y")


def units_kernel(ao_ref, chip_ref, slot_ref, three_ref, coef_ref, spread_ref, out_ref):
    step = pl.program_id(0)
    half = ao_ref[step] % 2
    rows = three_ref[0].astype(jnp.float32)
    tiles = rows.shape[1] // LANES
    stacked = [
        jnp.concatenate([rows[h * 8 : h * 8 + 8, j * LANES : (j + 1) * LANES] for j in range(tiles)], axis=0)
        for h in range(2)
    ]
    right = jnp.concatenate(stacked, axis=1).astype(jnp.bfloat16)
    depth = tiles * 8
    orbitals = coef_ref.shape[0]
    spread = jnp.dot(coef_ref[...], spread_ref[half], preferred_element_type=jnp.float32)
    lane = lax.broadcasted_iota(jnp.int32, (orbitals, 8, depth), 2)
    row = lax.broadcasted_iota(jnp.int32, (orbitals, 8, depth), 1)
    keep = (lane % 8) == row
    parts = []
    for parity in range(2):
        wide = jnp.broadcast_to(spread[:, None, parity * depth : (parity + 1) * depth], (orbitals, 8, depth))
        left = jnp.where(keep, wide, 0.0).reshape(orbitals * 8, depth).astype(jnp.bfloat16)
        made = jnp.dot(left, right, preferred_element_type=jnp.float32)
        parts.append(made.reshape(orbitals // 2, 2, 8, 2 * LANES))
    low = lax.broadcasted_iota(jnp.int32, (orbitals // 2, 8, LANES), 2) < BLK
    done = []
    for h in range(2):
        cut = slice(h * LANES, (h + 1) * LANES)
        stay = jnp.where(low, parts[0][:, 0, :, cut], parts[1][:, 1, :, cut])
        move = jnp.where(low, parts[0][:, 1, :, cut], parts[1][:, 0, :, cut])
        done.append(stay + pltpu.roll(move, BLK, 2))
    units = jnp.stack(done, axis=1).reshape(orbitals * 8, LANES).astype(jnp.bfloat16)
    out_ref[0, :, 0] = units.reshape(8, orbitals, LANES)


def make_units(three_center, coefficients, ao_block, chip, slot, chips):
    count, rows, depth = three_center.shape
    orbitals = coefficients.shape[0]
    wide = BLK // 2 * 8
    held = jnp.arange(LANES)[None, :, None]
    column = jnp.arange(2 * wide)[None, None, :]
    half = jnp.arange(2)[:, None, None]
    spread = (held == half * BLK + 2 * (column % wide // 8) + column // wide).astype(jnp.bfloat16)
    grid_spec = pltpu.PrefetchScalarGridSpec(
        num_scalar_prefetch=3,
        grid=(count,),
        in_specs=[
            pl.BlockSpec((1, rows, depth), lambda t, ao, chip, slot: (t, 0, 0)),
            pl.BlockSpec((orbitals, LANES), lambda t, ao, chip, slot: (0, ao[t] // 2)),
            pl.BlockSpec((2, LANES, 2 * wide), lambda t, ao, chip, slot: (0, 0, 0)),
        ],
        out_specs=pl.BlockSpec((1, 8, 1, orbitals, LANES), lambda t, ao, chip, slot: (chip[t], 0, slot[t], 0, 0)),
    )
    return pl.pallas_call(
        units_kernel,
        grid_spec=grid_spec,
        out_shape=jax.ShapeDtypeStruct((chips, 8, SLOTS, orbitals, LANES), jnp.bfloat16),
        name="units",
    )(ao_block, chip, slot, three_center, coefficients, spread)


def exchange_kernel(tag_ref, in_ref, metric_ref, out_ref, total, fitted):
    step = pl.program_id(0)
    sources, quarters, slots = in_ref.shape[0], in_ref.shape[1], in_ref.shape[2]

    @pl.when(step == 0)
    def _():
        total[...] = jnp.zeros_like(total)

    def add(k, carry):
        source, slot = k // slots, k % slots
        tag = tag_ref[step * sources + source, slot]

        @pl.when(tag >= 0)
        def _():
            owner, row, aux = tag // (ROWB * AUXB), tag // AUXB % ROWB, tag % AUXB
            for quarter in range(quarters):
                start = pl.multiple_of(row * BLK + quarter * 16, 16)
                for pair in range(2):
                    place = (owner, pair, aux, pl.ds(start, 16), slice(None))
                    total[place] += in_ref[source, quarter, slot, pair * 16 : pair * 16 + 16, :].astype(jnp.float32)

        return carry

    lax.fori_loop(0, sources * slots, add, 0)

    @pl.when(step == pl.num_programs(0) - 1)
    def _():
        for owner in range(2):
            for pair in range(2):
                whole = jnp.concatenate(
                    [total[owner, pair, aux].astype(jnp.bfloat16) for aux in range(AUXB)], axis=1
                )
                fitted[...] = jnp.dot(whole, metric_ref[...], preferred_element_type=jnp.float32).astype(jnp.bfloat16)
                part = lax.dot_general(
                    fitted[...], whole, (((1,), (1,)), ((), ())), preferred_element_type=jnp.float32
                )
                if pair == 0:
                    out_ref[owner] = part
                else:
                    out_ref[owner] += part


def make_exchange(tags, incoming, metric):
    sources, quarters, slots, rows, lanes = incoming.shape
    step = 4
    width = ROWB * BLK
    grid_spec = pltpu.PrefetchScalarGridSpec(
        num_scalar_prefetch=1,
        grid=(sources // step,),
        in_specs=[
            pl.BlockSpec((step, quarters, slots, rows, lanes), lambda s, tags: (s, 0, 0, 0, 0)),
            pl.BlockSpec(metric.shape, lambda s, tags: (0, 0)),
        ],
        out_specs=pl.BlockSpec((2, width, width), lambda s, tags: (0, 0, 0)),
        scratch_shapes=[
            pltpu.VMEM((2, 2, AUXB, width, lanes), jnp.float32),
            pltpu.VMEM((width, AUXB * lanes), jnp.bfloat16),
        ],
    )
    return pl.pallas_call(
        exchange_kernel,
        grid_spec=grid_spec,
        out_shape=jax.ShapeDtypeStruct((2, width, width), jnp.float32),
        compiler_params=pltpu.CompilerParams(vmem_limit_bytes=48 * 1024 * 1024),
        name="exchange",
    )(tags, incoming, metric)


def double_metric(metric_inv):
    blocks = metric_inv.reshape(AUXB, 1, BLK, AUXB, 1, BLK)
    same = jnp.eye(2, dtype=jnp.bool_).reshape(1, 2, 1, 1, 2, 1)
    return jnp.where(same, blocks, 0).reshape(2 * NAUX, 2 * NAUX)


def body(three_center, coefficients, metric_inv, target_owner, row_slot, aux_block, ao_block):
    count, rows, depth = three_center.shape
    orbitals = coefficients.shape[0]
    cores = lax.axis_size("c")
    chips = lax.axis_size("x") * lax.axis_size("z")
    target = target_owner[:, 0]
    chip, core = target // cores, target % cores
    code = core * (ROWB * AUXB) + row_slot * AUXB + aux_block
    counter = jnp.arange(count, dtype=jnp.int32)
    earlier = (chip[:, None] == chip[None, :]) & (counter[None, :] < counter[:, None])
    slot = jnp.sum(earlier.astype(jnp.int32), axis=1)
    placed = (jnp.arange(chips * SLOTS, dtype=jnp.int32)[:, None] == (chip * SLOTS + slot)[None, :])
    tags = jnp.max(jnp.where(placed, code[None, :], -1), axis=1).reshape(chips, 1, SLOTS)
    tags = jnp.broadcast_to(tags, (chips, cores, SLOTS)).reshape(chips * cores, SLOTS)
    tags = lax.all_to_all(tags, ("x", "z", "c"), split_axis=0, concat_axis=0, tiled=True)
    outgoing = make_units(three_center, coefficients, ao_block, chip, slot, chips)
    outgoing = outgoing.reshape(chips * 8, SLOTS, orbitals, LANES)
    incoming = lax.all_to_all(outgoing, AXES, split_axis=0, concat_axis=0, tiled=True)
    incoming = incoming.reshape(chips * cores, 4, SLOTS, orbitals, LANES)
    partial = make_exchange(tags, incoming, double_metric(metric_inv))
    width = ROWB * BLK
    share = width // 4
    partial = partial.reshape(cores * 4, share, width)
    partial = lax.all_to_all(partial, ("c", "y"), split_axis=0, concat_axis=0, tiled=True)
    return jnp.sum(partial, axis=0).astype(jnp.bfloat16)


def solution(mesh):
    split = Mesh(mesh.devices.reshape(4, 8, 2, 4), AXES)
    pair = ("x", "z", "c")
    in_specs = (P(pair, "y", None), P(), P(), P(pair, None), P(pair), P(pair), P(pair))
    out_specs = P(AXES, None)
    return jax.shard_map(body, mesh=split, in_specs=in_specs, out_specs=out_specs, check_vma=False)
```

time: 564 us -> 307 us (0.54)
  waiting for transfers between devices: 338 us -> 173 us
  local copies, waits for them, and re-layouts: 140 us -> 10.7 us
  Pallas kernels: 0 us -> 55.7 us
  matrix products: 43 us -> 0 us
  blocking collectives: 0 us -> 29.7 us
  between operations: 13.5 us -> 0.1 us
    all_gather x1 -> x0, waiting for transfers between devices: 153 us -> none  [body(): complete = lax.all_gather(gathered, 'fock', axis=1, tiled=True)]
    reshape x11 -> x0, local copies, waits for them, and re-layouts: 112 us -> none  [the longest x2 27.8 us: body(): summed.astype(jnp.bfloat16).reshape(ROWB, AUXB, rows_mine, orbitals, block)]
    pallas_call x0 -> x2, Pallas kernels: none -> 55.7 us  [the longest x1 35.1 us: make_units(): pl.pallas_call(units_kernel, grid_spec=grid_spec, out_shape=jax.ShapeDtyp...]
    dot_general x5 -> x0, matrix products: 43 us -> none  [the longest x1 13.4 us: body(): jnp.dot(left, complete.T, preferred_element_type=jnp.float32)]
    all_to_all x0 -> x1, blocking collectives: none -> 29.7 us  [body(): lax.all_to_all(partial, ('c', 'y'), split_axis=0, concat_axis=0, tiled=True)]
    unnamed x5 -> x6, local copies, waits for them, and re-layouts: 21.6 us -> 0.01 us
    all_to_all x2, waiting for transfers between devices: 184 us -> 173 us  [the longest x1 173 us: body(): lax.all_to_all(outgoing, AXES, split_axis=0, concat_axis=0, tiled=True)]
    select_n x0 -> x1, local copies, waits for them, and re-layouts: none -> 9.43 us  [double_metric(): return jnp.where(same, blocks, 0).reshape(2 * NAUX, 2 * NAUX)]
  transfers between devices with their start and end apart: 3 -> 2, of which waited for: 2 -> 1; matrix products, arithmetic and copies ran while one was open for 12% -> 5% of each run, Pallas kernels for 0% -> 12%
where the time goes in v1:
time: 307 us; the launch traced here: 305 us
  waiting for transfers between devices  173 us (56%)
  Pallas kernels  55.7 us (18%)
  blocking collectives  29.7 us (10%)
  starting transfers between devices  27 us (9%)
  local copies, waits for them, and re-layouts  10.7 us (3%)
  other arithmetic  9.02 us (3%)
    all_to_all x1, waiting for transfers between devices, body(): lax.all_to_all(outgoing, AXES, split_axis=0, concat_axis=0, tiled=True)  173 us
    pallas_call x1, Pallas kernels, make_units(): pl.pallas_call(units_kernel, grid_spec=grid_spec, out_shape=jax.ShapeDtyp...  35.1 us
    all_to_all x1, blocking collectives, body(): lax.all_to_all(partial, ('c', 'y'), split_axis=0, concat_axis=0, tiled=True)  29.7 us
    pallas_call x1, Pallas kernels, make_exchange(): pl.pallas_call(exchange_kernel, grid_spec=grid_spec, out_shape=jax.ShapeD...  20.6 us
    all_to_all x1, starting transfers between devices, body(): lax.all_to_all(outgoing, AXES, split_axis=0, concat_axis=0, tiled=True)  14 us
    all_to_all x1, starting transfers between devices, body(): lax.all_to_all(tags, ('x', 'z', 'c'), split_axis=0, concat_axis=0, tiled=...  13 us
    select_n x1, local copies, waits for them, and re-layouts, double_metric(): return jnp.where(same, blocks, 0).reshape(2 * NAUX, 2 * NAUX)  9.43 us
  transfers between devices with their start and end apart: 2, of which 1 were waited for; matrix products, arithmetic and copies ran while one was open for 5% of the time, Pallas kernels for 12%

profile of v1, /device:TPU:1, one launch (start us, length us, event | category | flops | bytes accessed | tf_op | source)
XLA Modules:
  0.0 305.3 jit_solution(11323022742608596888)
XLA Ops:
  0.0 0.7 fusion.14
  0.7 0.7 and_select_fusion.2
  1.4 0.0 copy-start.1
  1.4 0.2 convert_reduce_fusion.slot_ref
  1.6 0.0 copy-start.2
  1.6 0.1 select_reduce_fusion
  1.7 0.1 broadcast_in_dim.53
  1.8 0.6 broadcast_in_dim.54
  2.4 13.0 %all-to-all-start = ((s32[64,1,4]{2,1,0:T(1,128)}), s32[64,1,4]{2,1,0:T(1,128)S(1)}, u32[]{:S(2)}, u32[]{:S(2)}) async-start(s32[64,1,4]{2,1,0:T(1,128)} %bitcast.2), calls=%async_computation | async-start | bytes 65536 | tf_op jit(solution)/shard_map/all_to_all | solution.py:166
  15.4 0.1 add_add_fusion
  15.5 0.8 fusion.spread_ref
  16.3 0.0 copy-done.1
  16.3 0.0 copy-done.2
  16.3 35.1 %units.1 = bf16[32,8,4,32,128]{4,3,2,1,0:T(8,128)(2,1)} custom-call(s32[48]{0:T(128)} %ao_ref.1, s32[48]{0:T(128)} %copy-done.1, s32[48]{0:T(128)} %copy-done.2, bf16[48,16,4096]{2,1,0:T(8,128)(2,1)} %three_ref.1, bf16[32,19968]{1,0:T(8,128)(2,1)} %coef_ref.1, bf16[2,128,512]{2,1,0:T(8,128)(2,1)} %fusion.spread_ref), custom_call_target="tpu_custom_call" | custom-call | tf_op jit(solution)/shard_map/units/pallas_call | solution.py:70
  51.4 0.0 all-to-all-done
  51.4 0.0 copy-start
  51.4 14.0 %all-to-all-start.1 = ((bf16[256,4,32,128]{3,2,1,0:T(8,128)(2,1)}), bf16[256,4,32,128]{3,2,1,0:T(8,128)(2,1)}, u32[]{:S(2)}, u32[]{:S(2)}) async-start(bf16[256,4,32,128]{3,2,1,0:T(8,128)(2,1)} %bitcast.24), calls=%async_computation.1 | async-start | bytes 16777216 | tf_op jit(solution)/shard_map/all_to_all | solution.py:169
  65.5 0.0 copy-done
  65.5 0.5 broadcast_in_dim.56
  66.0 5.6 %broadcast_select_fusion = bf16[8,2,64,8,2,64]{5,4,3,2,1,0:T(2,128)(2,1)} fusion(pred[2,2]{1,0:T(4,128)(4,1)S(1)} %iota_compare_fusion.3, bf16[8,64,8,64]{3,2,1,0:T(8,128)(2,1)S(1)} %broadcast_in_dim.56), kind=kLoop, calls=%fused_computation | loop fusion | flops 1048576 | bytes 2621444 | tf_op jit(solution)/shard_map/jit(_where)/select_n | solution.py:149
  71.6 9.4 %select_n.63.metric_ref = bf16[1024,1024]{1,0:T(8,128)(2,1)S(1)} reshape(bf16[8,2,64,8,2,64]{5,4,3,2,1,0:T(2,128)(2,1)} %broadcast_select_fusion) | data formatting | bytes 4194304 | tf_op jit(solution)/shard_map/jit(_where)/select_n | solution.py:149
  81.1 173.0 %all-to-all-done.1 = bf16[256,4,32,128]{3,2,1,0:T(8,128)(2,1)} async-done(((bf16[256,4,32,128]{3,2,1,0:T(8,128)(2,1)}), bf16[256,4,32,128]{3,2,1,0:T(8,128)(2,1)}, u32[]{:S(2)}, u32[]{:S(2)}) %all-to-all-start.1) | async-done | bytes 8388640 | tf_op jit(solution)/shard_map/all_to_all | solution.py:169
  254.1 20.6 %exchange.1 = f32[2,512,512]{2,1,0:T(8,128)S(1)} custom-call(s32[64,4]{1,0:T(8,128)S(1)} %bitcast.23, bf16[64,4,4,32,128]{4,3,2,1,0:T(8,128)(2,1)} %bitcast.5.in_ref, bf16[1024,1024]{1,0:T(8,128)(2,1)S(1)} %select_n.63.metric_ref), custom_call_target="tpu_custom_call" | custom-call | tf_op jit(solution)/shard_map/exchange/pallas_call | solution.py:137
  274.7 29.7 %all_to_all.21 = f32[8,128,512]{2,1,0:T(8,128)S(1)} all-to-all(f32[8,128,512]{2,1,0:T(8,128)S(1)} %bitcast.22), channel_id=1, replica_groups=mesh['x'=4,'z'=8,'c'=2,'y'=4] {'c','y'}, dimensions={0} | all-to-all | bytes 4194304 | tf_op jit(solution)/shard_map/all_to_all | solution.py:175
  304.5 0.9 reduce_sum.19
  (4 shorter events, 0.0 us)
Async XLA Ops:
  1.4 14.9 %copy-start.1 = (s32[48]{0:T(128)}, s32[48]{0:T(128)S(1)}, u32[]{:S(2)}) copy-start(s32[48]{0:T(128)S(1)} %get-tuple-element.5.chip_ref) | copy-start | bytes 580
  1.6 14.7 %copy-start.2 = (s32[48]{0:T(128)}, s32[48]{0:T(128)S(1)}, u32[]{:S(2)}) copy-start(s32[48]{0:T(128)S(1)} %convert_reduce_fusion.slot_ref) | copy-start | bytes 580
  2.4 49.0 %all-to-all-start = ((s32[64,1,4]{2,1,0:T(1,128)}), s32[64,1,4]{2,1,0:T(1,128)S(1)}, u32[]{:S(2)}, u32[]{:S(2)}) async-start(s32[64,1,4]{2,1,0:T(1,128)} %bitcast.2), calls=%async_computation | async-start | bytes 65536 | tf_op jit(solution)/shard_map/all_to_all | solution.py:166
  51.4 14.0 %copy-start = (bf16[512,512]{1,0:T(8,128)(2,1)S(1)}, bf16[512,512]{1,0:T(8,128)(2,1)}, u32[]{:S(2)}) copy-start(bf16[512,512]{1,0:T(8,128)(2,1)} %param.9) | copy-start | bytes 1572868
  51.4 202.7 %all-to-all-start.1 = ((bf16[256,4,32,128]{3,2,1,0:T(8,128)(2,1)}), bf16[256,4,32,128]{3,2,1,0:T(8,128)(2,1)}, u32[]{:S(2)}, u32[]{:S(2)}) async-start(bf16[256,4,32,128]{3,2,1,0:T(8,128)(2,1)} %bitcast.24), calls=%async_computation.1 | async-start | bytes 16777216 | tf_op jit(solution)/shard_map/all_to_all | solution.py:169

commit v2 on v1

v2 whole, which is shorter than its diff:
```python
import functools

import jax
import jax.numpy as jnp
from jax import lax
from jax.experimental import pallas as pl
from jax.experimental.pallas import tpu as pltpu
from jax.sharding import Mesh, PartitionSpec as P

BLK = 64
AUXB = 8
ROWB = 8
NAUX = 512
LANES = 128
SLOTS = 4
AXES = ("x", "z", "c", "y")


def units_kernel(ao_ref, chip_ref, slot_ref, three_ref, coef_ref, spread_ref, out_ref, made_ref, sems):
    step = pl.program_id(0)
    group, _, depth_in = three_ref.shape
    tiles = depth_in // LANES
    depth = tiles * 8
    orbitals = coef_ref.shape[0]
    lane = lax.broadcasted_iota(jnp.int32, (orbitals, 8, depth), 2)
    row = lax.broadcasted_iota(jnp.int32, (orbitals, 8, depth), 1)
    keep = (lane % 8) == row
    low = lax.broadcasted_iota(jnp.int32, (orbitals // 2, 8, LANES), 2) < BLK

    def copy(unit):
        return pltpu.make_async_copy(
            made_ref.at[unit], out_ref.at[chip_ref[unit], :, slot_ref[unit]], sems.at[unit]
        )

    for k in range(group):
        unit = step * group + k
        ao = ao_ref[unit]
        rows = three_ref[k].astype(jnp.float32)
        stacked = [
            jnp.concatenate([rows[h * 8 : h * 8 + 8, j * LANES : (j + 1) * LANES] for j in range(tiles)], axis=0)
            for h in range(2)
        ]
        right = jnp.concatenate(stacked, axis=1).astype(jnp.bfloat16)
        picked = coef_ref[:, pl.ds(pl.multiple_of(ao // 2 * LANES, LANES), LANES)]
        spread = jnp.dot(picked, spread_ref[ao % 2], preferred_element_type=jnp.float32)
        parts = []
        for parity in range(2):
            wide = jnp.broadcast_to(spread[:, None, parity * depth : (parity + 1) * depth], (orbitals, 8, depth))
            left = jnp.where(keep, wide, 0.0).reshape(orbitals * 8, depth).astype(jnp.bfloat16)
            made = jnp.dot(left, right, preferred_element_type=jnp.float32)
            parts.append(made.reshape(orbitals // 2, 2, 8, 2 * LANES))
        done = []
        for h in range(2):
            cut = slice(h * LANES, (h + 1) * LANES)
            stay = jnp.where(low, parts[0][:, 0, :, cut], parts[1][:, 1, :, cut])
            move = jnp.where(low, parts[0][:, 1, :, cut], parts[1][:, 0, :, cut])
            done.append(stay + pltpu.roll(move, BLK, 2))
        units = jnp.stack(done, axis=1).reshape(orbitals * 8, LANES).astype(jnp.bfloat16)
        made_ref[unit] = units.reshape(8, orbitals, LANES)
        copy(unit).start()

    @pl.when(step == pl.num_programs(0) - 1)
    def _():
        for unit in range(made_ref.shape[0]):
            copy(unit).wait()


def make_units(three_center, coefficients, ao_block, chip, slot, chips):
    count, rows, depth = three_center.shape
    orbitals, functions = coefficients.shape
    wide = BLK // 2 * 8
    held = jnp.arange(LANES)[None, :, None]
    column = jnp.arange(2 * wide)[None, None, :]
    half = jnp.arange(2)[:, None, None]
    spread = (held == half * BLK + 2 * (column % wide // 8) + column // wide).astype(jnp.bfloat16)
    group = 4
    grid_spec = pltpu.PrefetchScalarGridSpec(
        num_scalar_prefetch=3,
        grid=(count // group,),
        in_specs=[
            pl.BlockSpec((group, rows, depth), lambda t, ao, chip, slot: (t, 0, 0)),
            pl.BlockSpec((orbitals, functions), lambda t, ao, chip, slot: (0, 0)),
            pl.BlockSpec((2, LANES, 2 * wide), lambda t, ao, chip, slot: (0, 0, 0)),
        ],
        out_specs=pl.BlockSpec(memory_space=pl.ANY),
        scratch_shapes=[
            pltpu.VMEM((count, 8, orbitals, LANES), jnp.bfloat16),
            pltpu.SemaphoreType.DMA((count,)),
        ],
    )
    return pl.pallas_call(
        units_kernel,
        grid_spec=grid_spec,
        out_shape=jax.ShapeDtypeStruct((chips, 8, SLOTS, orbitals, LANES), jnp.bfloat16),
        compiler_params=pltpu.CompilerParams(vmem_limit_bytes=32 * 1024 * 1024),
        name="units",
    )(ao_block, chip, slot, three_center, coefficients, spread)


def own_exchange(whole, metric_ref, fitted, out_ref, first):
    fitted[...] = jnp.dot(whole, metric_ref[...], preferred_element_type=jnp.float32).astype(jnp.bfloat16)
    part = lax.dot_general(fitted[...], whole, (((1,), (1,)), ((), ())), preferred_element_type=jnp.float32)
    if first:
        out_ref[...] = part
    else:
        out_ref[...] += part


def gather_kernel(tag_ref, core_ref, in_ref, metric_ref, mine_ref, out_ref, total, fitted):
    step = pl.program_id(0)
    sources, quarters, slots = in_ref.shape[0], in_ref.shape[1], in_ref.shape[2]

    @pl.when(step == 0)
    def _():
        total[...] = jnp.zeros_like(total)

    def add(k, carry):
        source, slot = k // slots, k % slots
        tag = tag_ref[step * sources + source, slot]

        @pl.when(tag >= 0)
        def _():
            owner, row, aux = tag // (ROWB * AUXB), tag // AUXB % ROWB, tag % AUXB
            places = [
                (owner, pair, aux, pl.ds(pl.multiple_of(row * BLK + quarter * 16, 16), 16), slice(None))
                for quarter in range(quarters)
                for pair in range(2)
            ]
            news = [
                in_ref[source, quarter, slot, pair * 16 : pair * 16 + 16, :].astype(jnp.float32)
                for quarter in range(quarters)
                for pair in range(2)
            ]
            sums = [total[place] + new for place, new in zip(places, news)]
            for place, value in zip(places, sums):
                total[place] = value

        return carry

    lax.fori_loop(0, sources * slots, add, 0)

    @pl.when(step == pl.num_programs(0) - 1)
    def _():
        mine = core_ref[0]
        for pair in range(2):
            whole = [total[1 - mine, pair, aux].astype(jnp.bfloat16) for aux in range(AUXB)]
            own_exchange(jnp.concatenate(whole, axis=1), metric_ref, fitted, out_ref, pair == 0)
        for pair in range(2):
            for aux in range(AUXB):
                mine_ref[pair, :, aux * LANES : (aux + 1) * LANES] = total[mine, pair, aux].astype(jnp.bfloat16)


def rest_kernel(mine_ref, metric_ref, out_ref, fitted):
    for pair in range(2):
        own_exchange(mine_ref[pair], metric_ref, fitted, out_ref, pair == 0)


def make_exchange(tags, core, incoming, metric):
    sources, quarters, slots, rows, lanes = incoming.shape
    step = 16
    width = ROWB * BLK
    inner = AUXB * lanes
    grid_spec = pltpu.PrefetchScalarGridSpec(
        num_scalar_prefetch=2,
        grid=(sources // step,),
        in_specs=[
            pl.BlockSpec((step, quarters, slots, rows, lanes), lambda s, tags, core: (s, 0, 0, 0, 0)),
            pl.BlockSpec(metric.shape, lambda s, tags, core: (0, 0)),
        ],
        out_specs=[
            pl.BlockSpec((2, width, inner), lambda s, tags, core: (0, 0, 0)),
            pl.BlockSpec((width, width), lambda s, tags, core: (0, 0)),
        ],
        scratch_shapes=[
            pltpu.VMEM((2, 2, AUXB, width, lanes), jnp.float32),
            pltpu.VMEM((width, inner), jnp.bfloat16),
        ],
    )
    params = pltpu.CompilerParams(vmem_limit_bytes=48 * 1024 * 1024)
    mine, sent = pl.pallas_call(
        gather_kernel,
        grid_spec=grid_spec,
        out_shape=[
            jax.ShapeDtypeStruct((2, width, inner), jnp.bfloat16),
            jax.ShapeDtypeStruct((width, width), jnp.float32),
        ],
        compiler_params=params,
        name="gather_exchange",
    )(tags, core, incoming, metric)
    got = lax.ppermute(sent, "c", [(0, 1), (1, 0)])
    flops = 4 * width * inner * (inner + width)
    held = pl.pallas_call(
        rest_kernel,
        out_shape=jax.ShapeDtypeStruct((width, width), jnp.float32),
        scratch_shapes=[pltpu.VMEM((width, inner), jnp.bfloat16)],
        compiler_params=params,
        cost_estimate=pl.CostEstimate(flops=flops, bytes_accessed=5 * width * inner * 2, transcendentals=0),
        name="own_exchange",
    )(mine, metric)
    return held + got


def double_metric(metric_inv):
    blocks = metric_inv.reshape(AUXB, 1, BLK, AUXB, 1, BLK)
    same = jnp.eye(2, dtype=jnp.bool_).reshape(1, 2, 1, 1, 2, 1)
    return jnp.where(same, blocks, 0).reshape(2 * NAUX, 2 * NAUX)


def body(three_center, coefficients, metric_inv, target_owner, row_slot, aux_block, ao_block):
    count, rows, depth = three_center.shape
    orbitals = coefficients.shape[0]
    cores = lax.axis_size("c")
    chips = lax.axis_size("x") * lax.axis_size("z")
    target = target_owner[:, 0]
    chip, core = target // cores, target % cores
    code = core * (ROWB * AUXB) + row_slot * AUXB + aux_block
    counter = jnp.arange(count, dtype=jnp.int32)
    earlier = (chip[:, None] == chip[None, :]) & (counter[None, :] < counter[:, None])
    slot = jnp.sum(earlier.astype(jnp.int32), axis=1)
    placed = (jnp.arange(chips * SLOTS, dtype=jnp.int32)[:, None] == (chip * SLOTS + slot)[None, :])
    tags = jnp.max(jnp.where(placed, code[None, :], -1), axis=1).reshape(1, chips * SLOTS)
    tags = tags.astype(jnp.bfloat16)
    tags = lax.all_gather(tags, ("x", "z", "c"), axis=0, tiled=True)
    my_chip = lax.axis_index("x") * lax.axis_size("z") + lax.axis_index("z")
    tags = lax.dynamic_slice_in_dim(tags, my_chip * SLOTS, SLOTS, 1).astype(jnp.int32)
    my_core = lax.axis_index("c").reshape(1)
    outgoing = make_units(three_center, coefficients, ao_block, chip, slot, chips)
    outgoing = outgoing.reshape(chips * 8, SLOTS, orbitals, LANES)
    incoming = lax.all_to_all(outgoing, AXES, split_axis=0, concat_axis=0, tiled=True)
    incoming = incoming.reshape(chips * cores, 4, SLOTS, orbitals, LANES)
    partial = make_exchange(tags, my_core, incoming, double_metric(metric_inv))
    width = ROWB * BLK
    partial = partial.reshape(4, width // 4, width)
    partial = lax.all_to_all(partial, "y", split_axis=0, concat_axis=0, tiled=True)
    return jnp.sum(partial, axis=0).astype(jnp.bfloat16)


def solution(mesh):
    split = Mesh(mesh.devices.reshape(4, 8, 2, 4), AXES)
    pair = ("x", "z", "c")
    in_specs = (P(pair, "y", None), P(), P(), P(pair, None), P(pair), P(pair), P(pair))
    out_specs = P(AXES, None)
    return jax.shard_map(body, mesh=split, in_specs=in_specs, out_specs=out_specs, check_vma=False)
```

time: 307 us -> 302 us (0.984)
  blocking collectives: 29.7 us -> 218 us
  waiting for transfers between devices: 173 us -> 0.01 us
  Pallas kernels: 55.7 us -> 41.2 us
  starting transfers between devices: 27 us -> 16.9 us
  local copies, waits for them, and re-layouts: 10.7 us -> 18 us
    all_gather x0 -> x1, blocking collectives: none -> 199 us  [body(): tags = lax.all_gather(tags, ('x', 'z', 'c'), axis=0, tiled=True)]
    all_to_all x1, waiting for transfers between devices: 173 us -> 0.01 us  [body(): lax.all_to_all(outgoing, AXES, split_axis=0, concat_axis=0, tiled=True)]
    pallas_call x1, Pallas kernels: 35.1 us -> 21.9 us  [make_units(): pl.pallas_call(units_kernel, grid_spec=grid_spec, out_shape=jax.ShapeDtyp...]
    all_to_all x1 -> x0, starting transfers between devices: 13 us -> none  [body(): lax.all_to_all(tags, ('x', 'z', 'c'), split_axis=0, concat_axis=0, tiled=...]
    all_to_all x1, blocking collectives: 29.7 us -> 18.1 us  [body(): lax.all_to_all(partial, 'y', split_axis=0, concat_axis=0, tiled=True)]
    unnamed x6 -> x10, local copies, waits for them, and re-layouts: 0.01 us -> 7.97 us
    pallas_call x1 -> x2, Pallas kernels: 20.6 us -> 19.3 us  [the longest x1 15.9 us: make_exchange(): pl.pallas_call(gather_kernel, grid_spec=grid_spec, out_shape=[jax.ShapeDt...]
  transfers between devices with their start and end apart: 2 -> 2, of which waited for: 1 -> 0; matrix products, arithmetic and copies ran while one was open for 5% -> 5% of each run, Pallas kernels for 12% -> 1%
where the time goes in v2:
time: 302 us
  blocking collectives  218 us (72%)
  Pallas kernels  41.2 us (14%)
  local copies, waits for them, and re-layouts  18 us (6%)
  starting transfers between devices  16.9 us (6%)
  other arithmetic  8.4 us (3%)
    all_gather x1, blocking collectives, body(): tags = lax.all_gather(tags, ('x', 'z', 'c'), axis=0, tiled=True)  199 us
    pallas_call x1, Pallas kernels, make_units(): pl.pallas_call(units_kernel, grid_spec=grid_spec, out_shape=jax.ShapeDtyp...  21.9 us
    all_to_all x1, blocking collectives, body(): lax.all_to_all(partial, 'y', split_axis=0, concat_axis=0, tiled=True)  18.1 us
    all_to_all x1, starting transfers between devices, body(): lax.all_to_all(outgoing, AXES, split_axis=0, concat_axis=0, tiled=True)  16.7 us
    pallas_call x1, Pallas kernels, make_exchange(): pl.pallas_call(gather_kernel, grid_spec=grid_spec, out_shape=[jax.ShapeDt...  15.9 us
    select_n x1, local copies, waits for them, and re-layouts, double_metric(): return jnp.where(same, blocks, 0).reshape(2 * NAUX, 2 * NAUX)  9.43 us
    unnamed x10, local copies, waits for them, and re-layouts  7.97 us
  transfers between devices with their start and end apart: 2, of which 0 were waited for; matrix products, arithmetic and copies ran while one was open for 5% of the time, Pallas kernels for 1%

profile of v2, /device:TPU:1, one launch (start us, length us, event | category | flops | bytes accessed | tf_op | source)
XLA Modules:
  0.0 302.3 jit_solution(3761583417436770957)
XLA Ops:
  0.0 0.7 fusion.15
  0.7 0.1 add_add_fusion
  0.8 0.1 fusion.spread_ref
  0.8 0.7 and_select_fusion.2
  1.5 0.2 convert_reduce_fusion.slot_ref
  1.7 0.0 copy-start.1
  1.7 2.8 copy-done.1
  4.5 0.0 copy-start.2
  4.5 1.3 copy-done.2
  5.8 0.0 copy-start.3
  5.8 0.7 copy-done.3
  6.4 21.9 %units.1 = bf16[32,8,4,32,128]{4,3,2,1,0:T(8,128)(2,1)S(1)} custom-call(s32[48]{0:T(128)S(1)} %copy-done.3, s32[48]{0:T(128)S(1)} %get-tuple-element.9.chip_ref, s32[48]{0:T(128)S(1)} %convert_reduce_fusion.slot_ref, bf16[48,16,4096]{2,1,0:T(8,128)(2,1)S(1)} %copy-done.1, bf16[32,19968]{1,0:T(8,128)(2,1)S(1)} %copy-done.2, ...), custom_call_target="tpu_custom_call" | custom-call | tf_op jit(solution)/shard_map/units/pallas_call | solution.py:91
  28.4 0.0 copy-start
  28.4 3.2 %copy-done = bf16[32,8,4,32,128]{4,3,2,1,0:T(8,128)(2,1)} copy-done((bf16[32,8,4,32,128]{4,3,2,1,0:T(8,128)(2,1)}, bf16[32,8,4,32,128]{4,3,2,1,0:T(8,128)(2,1)S(1)}, u32[]{:S(2)}) %copy-start) | copy-done | bytes 8388632
  31.6 0.0 copy-start.4
  31.6 16.7 %all-to-all-start = ((bf16[256,4,32,128]{3,2,1,0:T(8,128)(2,1)}), bf16[256,4,32,128]{3,2,1,0:T(8,128)(2,1)}, u32[]{:S(2)}, u32[]{:S(2)}) async-start(bf16[256,4,32,128]{3,2,1,0:T(8,128)(2,1)} %bitcast.28), calls=%async_computation | async-start | bytes 16777216 | tf_op jit(solution)/shard_map/all_to_all | solution.py:229
  48.3 0.0 copy-done.4
  48.3 0.5 broadcast_in_dim.47
  48.8 5.6 %broadcast_select_fusion = bf16[8,2,64,8,2,64]{5,4,3,2,1,0:T(2,128)(2,1)} fusion(pred[2,2]{1,0:T(4,128)(4,1)S(1)} %iota_compare_fusion.3, bf16[8,64,8,64]{3,2,1,0:T(8,128)(2,1)S(1)} %broadcast_in_dim.47), kind=kLoop, calls=%fused_computation | loop fusion | flops 1048576 | bytes 2621444 | tf_op jit(solution)/shard_map/jit(_where)/select_n | solution.py:206
  54.4 9.4 %select_n.67.metric_ref = bf16[1024,1024]{1,0:T(8,128)(2,1)S(1)} reshape(bf16[8,2,64,8,2,64]{5,4,3,2,1,0:T(2,128)(2,1)} %broadcast_select_fusion) | data formatting | bytes 4194304 | tf_op jit(solution)/shard_map/jit(_where)/select_n | solution.py:206
  63.9 0.1 select_reduce_fusion
  64.0 199.5 %all-gather.1 = bf16[64,1,128]{2,1,0:T(2,128)(2,1)S(1)} all-gather(bf16[1,1,128]{2,1,0:T(2,128)(2,1)S(1)} %convert_bitcast_fusion), channel_id=2, replica_groups=mesh['x'=4,'z'=8,'c'=2,'y'=4] {'x','z','c'}, dimensions={0}, use_global_device_ids=true | all-gather | bytes 16640 | tf_op jit(solution)/shard_map/all_gather | solution.py:223
  263.5 0.1 constant_dynamic-slice_fusion
  263.6 0.0 all-to-all-done
  263.6 15.9 %gather_exchange.1 = (bf16[2,512,1024]{2,1,0:T(8,128)(2,1)S(1)}, f32[512,512]{1,0:T(8,128)S(1)}) custom-call(s32[64,4]{1,0:T(8,128)S(1)} %fusion.2.tag_ref, s32[1]{0:T(128)} %bitcast.4.core_ref, bf16[64,4,4,32,128]{4,3,2,1,0:T(8,128)(2,1)} %bitcast.6.in_ref, bf16[1024,1024]{1,0:T(8,128)(2,1)S(1)} %select_n.67.metric_ref), custom_call_target="tpu_custom_call" | custom-call | tf_op jit(solution)/shard_map/gather_exchange/pallas_call | solution.py:180
  279.5 0.3 collective-permute-start
  279.8 3.4 %own_exchange.1 = f32[512,512]{1,0:T(8,128)S(1)} custom-call(bf16[2,512,1024]{2,1,0:T(8,128)(2,1)S(1)} %get-tuple-element.7.mine_ref, bf16[1024,1024]{1,0:T(8,128)(2,1)S(1)} %select_n.67.metric_ref), custom_call_target="tpu_custom_call" | custom-call | flops 3221225472 | bytes 5242880 | tf_op jit(solution)/shard_map/own_exchange/pallas_call | solution.py:192
  283.2 0.0 collective-permute-done
  283.2 0.2 add.103
  283.4 18.1 %all_to_all.10 = f32[4,128,512]{2,1,0:T(8,128)S(1)} all-to-all(f32[4,128,512]{2,1,0:T(8,128)S(1)} %bitcast.29), channel_id=1, replica_groups=mesh['x'=4,'z'=8,'c'=2,'y'=4] {'y'}, dimensions={0} | all-to-all | bytes 2097152 | tf_op jit(solution)/shard_map/all_to_all | solution.py:234
  301.5 0.8 reduce_sum.19
  (6 shorter events, 0.0 us)
Async XLA Ops:
  1.7 2.8 copy-start.1
  4.5 1.3 copy-start.2
  5.8 0.7 copy-start.3
  28.4 3.2 %copy-start = (bf16[32,8,4,32,128]{4,3,2,1,0:T(8,128)(2,1)}, bf16[32,8,4,32,128]{4,3,2,1,0:T(8,128)(2,1)S(1)}, u32[]{:S(2)}) copy-start(bf16[32,8,4,32,128]{4,3,2,1,0:T(8,128)(2,1)S(1)} %units.1) | copy-start | bytes 25165828
  31.6 16.7 %copy-start.4 = (bf16[512,512]{1,0:T(8,128)(2,1)S(1)}, bf16[512,512]{1,0:T(8,128)(2,1)}, u32[]{:S(2)}) copy-start(bf16[512,512]{1,0:T(8,128)(2,1)} %param.9) | copy-start | bytes 1572868
  31.6 232.0 %all-to-all-start = ((bf16[256,4,32,128]{3,2,1,0:T(8,128)(2,1)}), bf16[256,4,32,128]{3,2,1,0:T(8,128)(2,1)}, u32[]{:S(2)}, u32[]{:S(2)}) async-start(bf16[256,4,32,128]{3,2,1,0:T(8,128)(2,1)} %bitcast.28), calls=%async_computation | async-start | bytes 16777216 | tf_op jit(solution)/shard_map/all_to_all | solution.py:229
  279.5 3.7 %collective-permute-start = (f32[512,512]{1,0:T(8,128)S(1)}, f32[512,512]{1,0:T(8,128)S(1)}, u32[]{:S(2)}, u32[]{:S(2)}) collective-permute-start(f32[512,512]{1,0:T(8,128)S(1)} %get-tuple-element.8), channel_id=1, source_target_pairs={{0,4},{4,0},{1,5},{5,1},{2,6},{6,2},{3,7},{7,3},{8,12},{12,8},{9,1... | collective-permute-start | bytes 3145736 | tf_op jit(solution)/shard_map/ppermute | solution.py:190

commit v3 on v2

v3 whole, which is shorter than its diff:
```python
import functools

import jax
import jax.numpy as jnp
from jax import lax
from jax.experimental import pallas as pl
from jax.experimental.pallas import tpu as pltpu
from jax.sharding import Mesh, PartitionSpec as P

BLK = 64
AUXB = 8
ROWB = 8
NAUX = 512
LANES = 128
SLOTS = 4
MAIN = 3
GROUP = 4
PART = 16
AXES = ("x", "z", "c", "y")


def units_kernel(ao_ref, chip_ref, slot_ref, three_ref, coef_ref, spread_ref, main_ref, extra_ref, rows_ref, made_ref, got, sent):
    count, _, depth_in = rows_ref.shape
    tiles = depth_in // LANES
    depth = tiles * 8
    orbitals = coef_ref.shape[0]
    lane = lax.broadcasted_iota(jnp.int32, (orbitals, 8, depth), 2)
    row = lax.broadcasted_iota(jnp.int32, (orbitals, 8, depth), 1)
    keep = (lane % 8) == row
    low = lax.broadcasted_iota(jnp.int32, (orbitals // 2, 8, LANES), 2) < BLK

    def fetch(step):
        units = pl.ds(step * GROUP, GROUP)
        return pltpu.make_async_copy(three_ref.at[units], rows_ref.at[units], got.at[step])

    def send(unit, act):
        chip, slot = chip_ref[unit], slot_ref[unit]

        @pl.when(slot < MAIN)
        def _():
            act(pltpu.make_async_copy(made_ref.at[unit], main_ref.at[chip, :, slot], sent.at[unit]))

        @pl.when(slot >= MAIN)
        def _():
            act(pltpu.make_async_copy(made_ref.at[unit], extra_ref.at[chip, :, 0], sent.at[unit]))

    for step in range(count // GROUP):
        fetch(step).start()

    def group(step, carry):
        fetch(step).wait()
        spreads, rights = [], []
        for k in range(GROUP):
            ao = ao_ref[step * GROUP + k]
            picked = coef_ref[:, pl.ds(pl.multiple_of(ao // 2 * LANES, LANES), LANES)]
            spreads.append(jnp.dot(picked, spread_ref[ao % 2], preferred_element_type=jnp.float32))
        for k in range(GROUP):
            rows = rows_ref[step * GROUP + k].astype(jnp.float32)
            stacked = [
                jnp.concatenate([rows[h * 8 : h * 8 + 8, j * LANES : (j + 1) * LANES] for j in range(tiles)], axis=0)
                for h in range(2)
            ]
            right = jnp.concatenate(stacked, axis=1).astype(jnp.bfloat16)
            parts = []
            for parity in range(2):
                wide = spreads[k][:, None, parity * depth : (parity + 1) * depth]
                wide = jnp.broadcast_to(wide, (orbitals, 8, depth))
                left = jnp.where(keep, wide, 0.0).reshape(orbitals * 8, depth).astype(jnp.bfloat16)
                made = jnp.dot(left, right, preferred_element_type=jnp.float32)
                parts.append(made.reshape(orbitals // 2, 2, 8, 2 * LANES))
            done = []
            for h in range(2):
                cut = slice(h * LANES, (h + 1) * LANES)
                stay = jnp.where(low, parts[0][:, 0, :, cut], parts[1][:, 1, :, cut])
                move = jnp.where(low, parts[0][:, 1, :, cut], parts[1][:, 0, :, cut])
                done.append(stay + pltpu.roll(move, BLK, 2))
            units = jnp.stack(done, axis=1).reshape(orbitals * 8, LANES).astype(jnp.bfloat16)
            made_ref[step * GROUP + k] = units.reshape(8, orbitals, LANES)
        for k in range(GROUP):
            send(step * GROUP + k, lambda copy: copy.start())
        return carry

    lax.fori_loop(0, count // GROUP, group, 0)
    for unit in range(count):
        send(unit, lambda copy: copy.wait())


def make_units(three_center, coefficients, ao_block, chip, slot, chips):
    count, rows, depth = three_center.shape
    orbitals = coefficients.shape[0]
    wide = BLK // 2 * 8
    held = jnp.arange(LANES)[None, :, None]
    column = jnp.arange(2 * wide)[None, None, :]
    half = jnp.arange(2)[:, None, None]
    spread = (held == half * BLK + 2 * (column % wide // 8) + column // wide).astype(jnp.bfloat16)
    scalars = pl.BlockSpec(memory_space=pltpu.SMEM)
    return pl.pallas_call(
        units_kernel,
        in_specs=[scalars] * 3
        + [pl.BlockSpec(memory_space=pltpu.HBM)]
        + [pl.BlockSpec(memory_space=pltpu.VMEM)] * 2,
        out_specs=[pl.BlockSpec(memory_space=pltpu.HBM)] * 2,
        out_shape=[
            jax.ShapeDtypeStruct((chips, 8, MAIN, orbitals, LANES), jnp.bfloat16),
            jax.ShapeDtypeStruct((chips, 8, SLOTS - MAIN, orbitals, LANES), jnp.bfloat16),
        ],
        scratch_shapes=[
            pltpu.VMEM((count, rows, depth), jnp.bfloat16),
            pltpu.VMEM((count, 8, orbitals, LANES), jnp.bfloat16),
            pltpu.SemaphoreType.DMA((count // GROUP,)),
            pltpu.SemaphoreType.DMA((count,)),
        ],
        compiler_params=pltpu.CompilerParams(vmem_limit_bytes=60 * 1024 * 1024),
        name="units",
    )(ao_block, chip, slot, three_center, coefficients, spread)


def own_exchange(whole, metric_ref, fitted, out_ref, first):
    fitted[...] = jnp.dot(whole, metric_ref[...], preferred_element_type=jnp.float32).astype(jnp.bfloat16)
    part = lax.dot_general(fitted[...], whole, (((1,), (1,)), ((), ())), preferred_element_type=jnp.float32)
    if first:
        out_ref[...] = part
    else:
        out_ref[...] += part


def gather_kernel(list_ref, filled_ref, core_ref, in_ref, metric_ref, mine_ref, out_ref, total, fitted):
    step = pl.program_id(0)
    quarters, slots = in_ref.shape[1], in_ref.shape[2]

    @pl.when(step == 0)
    def _():
        total[...] = jnp.zeros_like(total)

    def add(k, carry):
        entry = list_ref[step, k]
        spot, tag = entry // (2 * ROWB * AUXB), entry % (2 * ROWB * AUXB)
        source, slot = spot // slots, spot % slots
        owner, row, aux = tag // (ROWB * AUXB), tag // AUXB % ROWB, tag % AUXB
        places = [
            (owner, pair, aux, pl.ds(pl.multiple_of(row * BLK + quarter * 16, 16), 16), slice(None))
            for quarter in range(quarters)
            for pair in range(2)
        ]
        news = [
            in_ref[source, quarter, slot, pair * 16 : pair * 16 + 16, :].astype(jnp.float32)
            for quarter in range(quarters)
            for pair in range(2)
        ]
        sums = [total[place] + new for place, new in zip(places, news)]
        for place, value in zip(places, sums):
            total[place] = value
        return carry

    lax.fori_loop(0, filled_ref[step], add, 0)

    @pl.when(step == pl.num_programs(0) - 1)
    def _():
        mine = core_ref[0]
        for pair in range(2):
            whole = [total[1 - mine, pair, aux].astype(jnp.bfloat16) for aux in range(AUXB)]
            own_exchange(jnp.concatenate(whole, axis=1), metric_ref, fitted, out_ref, pair == 0)
        for pair in range(2):
            for aux in range(AUXB):
                mine_ref[pair, :, aux * LANES : (aux + 1) * LANES] = total[mine, pair, aux].astype(jnp.bfloat16)


def rest_kernel(mine_ref, metric_ref, out_ref, fitted):
    for pair in range(2):
        own_exchange(mine_ref[pair], metric_ref, fitted, out_ref, pair == 0)


def filled_list(tags):
    sources, slots = tags.shape
    tags = tags.reshape(sources // PART, PART * slots)
    filled = tags >= 0
    spot = jnp.arange(PART * slots, dtype=jnp.int32)
    before = spot[:, None] < spot[None, :]
    place = jnp.sum((filled[:, :, None] & before[None]).astype(jnp.int32), axis=1)
    here = filled[:, :, None] & (place[:, :, None] == spot)
    entry = spot * (2 * ROWB * AUXB) + tags
    return jnp.sum(jnp.where(here, entry[:, :, None], 0), axis=1), jnp.sum(filled.astype(jnp.int32), axis=1)


def gather_exchange(entries, filled, core, incoming, metric):
    sources, quarters, slots, rows, lanes = incoming.shape
    width = ROWB * BLK
    inner = AUXB * lanes
    grid_spec = pltpu.PrefetchScalarGridSpec(
        num_scalar_prefetch=3,
        grid=(sources // PART,),
        in_specs=[
            pl.BlockSpec((PART, quarters, slots, rows, lanes), lambda s, entries, filled, core: (s, 0, 0, 0, 0)),
            pl.BlockSpec(metric.shape, lambda s, entries, filled, core: (0, 0)),
        ],
        out_specs=[
            pl.BlockSpec((2, width, inner), lambda s, entries, filled, core: (0, 0, 0)),
            pl.BlockSpec((width, width), lambda s, entries, filled, core: (0, 0)),
        ],
        scratch_shapes=[
            pltpu.VMEM((2, 2, AUXB, width, lanes), jnp.float32),
            pltpu.VMEM((width, inner), jnp.bfloat16),
        ],
    )
    return pl.pallas_call(
        gather_kernel,
        grid_spec=grid_spec,
        out_shape=[
            jax.ShapeDtypeStruct((2, width, inner), jnp.bfloat16),
            jax.ShapeDtypeStruct((width, width), jnp.float32),
        ],
        compiler_params=pltpu.CompilerParams(vmem_limit_bytes=48 * 1024 * 1024),
        name="gather_exchange",
    )(entries, filled, core, incoming, metric)


def rest_exchange(mine, metric):
    _, width, inner = mine.shape
    flops = 4 * width * inner * (inner + width)
    return pl.pallas_call(
        rest_kernel,
        out_shape=jax.ShapeDtypeStruct((width, width), jnp.float32),
        scratch_shapes=[pltpu.VMEM((width, inner), jnp.bfloat16)],
        compiler_params=pltpu.CompilerParams(vmem_limit_bytes=48 * 1024 * 1024),
        cost_estimate=pl.CostEstimate(flops=flops, bytes_accessed=5 * width * inner * 2, transcendentals=0),
        name="own_exchange",
    )(mine, metric)


def double_metric(metric_inv):
    blocks = metric_inv.reshape(AUXB, 1, BLK, AUXB, 1, BLK)
    same = jnp.eye(2, dtype=jnp.bool_).reshape(1, 2, 1, 1, 2, 1)
    return jnp.where(same, blocks, 0).reshape(2 * NAUX, 2 * NAUX)


def body(three_center, coefficients, metric_inv, target_owner, row_slot, aux_block, ao_block):
    count, rows, depth = three_center.shape
    orbitals = coefficients.shape[0]
    cores = lax.axis_size("c")
    chips = lax.axis_size("x") * lax.axis_size("z")
    target = target_owner[:, 0]
    chip, core = target // cores, target % cores
    code = core * (ROWB * AUXB) + row_slot * AUXB + aux_block
    counter = jnp.arange(count, dtype=jnp.int32)
    earlier = (chip[:, None] == chip[None, :]) & (counter[None, :] < counter[:, None])
    slot = jnp.sum(earlier.astype(jnp.int32), axis=1)
    placed = (jnp.arange(chips * SLOTS, dtype=jnp.int32)[:, None] == (chip * SLOTS + slot)[None, :])
    tags = jnp.max(jnp.where(placed, code[None, :], -1), axis=1).reshape(chips, SLOTS)
    more = jnp.broadcast_to(jnp.max(tags[:, MAIN:]), (chips, 1))
    tags = jnp.concatenate([tags, more], axis=1)[:, None]
    tags = jnp.broadcast_to(tags, (chips, cores, SLOTS + 1)).reshape(chips * cores, SLOTS + 1)
    tags = lax.all_to_all(tags, ("x", "z", "c"), split_axis=0, concat_axis=0, tiled=True)
    my_core = lax.axis_index("c").reshape(1)
    main, extra = make_units(three_center, coefficients, ao_block, chip, slot, chips)
    main = main.reshape(chips * 8, MAIN, orbitals, LANES)
    extra = extra.reshape(chips * 8, SLOTS - MAIN, orbitals, LANES)
    main = lax.all_to_all(main, AXES, split_axis=0, concat_axis=0, tiled=True)
    metric = double_metric(metric_inv)

    few_list, many_list = lax.optimization_barrier((filled_list(tags[:, :MAIN]), filled_list(tags[:, :SLOTS])))

    def few(main, extra, few_list, many_list, core, metric):
        main = main.reshape(chips * cores, 4, MAIN, orbitals, LANES)
        return gather_exchange(*few_list, core, main, metric)

    def many(main, extra, few_list, many_list, core, metric):
        extra = lax.all_to_all(extra, AXES, split_axis=0, concat_axis=0, tiled=True)
        both = jnp.concatenate([main, extra], axis=1).reshape(chips * cores, 4, SLOTS, orbitals, LANES)
        return gather_exchange(*many_list, core, both, metric)

    overflow = jnp.max(tags[:, SLOTS]) >= 0
    mine, sent = lax.cond(overflow, many, few, main, extra, few_list, many_list, my_core, metric)
    got = lax.ppermute(sent, "c", [(0, 1), (1, 0)])
    partial = rest_exchange(mine, metric) + got
    width = ROWB * BLK
    partial = partial.reshape(4, width // 4, width)
    partial = lax.all_to_all(partial, "y", split_axis=0, concat_axis=0, tiled=True)
    return jnp.sum(partial, axis=0).astype(jnp.bfloat16)


def solution(mesh):
    split = Mesh(mesh.devices.reshape(4, 8, 2, 4), AXES)
    pair = ("x", "z", "c")
    in_specs = (P(pair, "y", None), P(), P(), P(pair, None), P(pair), P(pair), P(pair))
    out_specs = P(AXES, None)
    return jax.shard_map(body, mesh=split, in_specs=in_specs, out_specs=out_specs, check_vma=False)
```

time: 302 us -> 223 us (0.74)
  blocking collectives: 218 us -> 17.4 us
  waiting for transfers between devices: 0.01 us -> 125 us
  Pallas kernels: 41.2 us -> 28.1 us
  starting transfers between devices: 16.9 us -> 27.9 us
  local copies, waits for them, and re-layouts: 18 us -> 11.7 us
  other arithmetic: 8.4 us -> 11.6 us
    all_gather x1 -> x0, blocking collectives: 199 us -> none  [body(): tags = lax.all_gather(tags, ('x', 'z', 'c'), axis=0, tiled=True)]
    all_to_all x1 -> x2, waiting for transfers between devices: 0.01 us -> 125 us  [the longest x1 125 us: body(): main = lax.all_to_all(main, AXES, split_axis=0, concat_axis=0, tiled=True)]
    pallas_call x3, Pallas kernels: 41.2 us -> 28.1 us  [the longest x1 11.6 us: gather_exchange(): pl.pallas_call(gather_kernel, grid_spec=grid_spec, out_shape=[jax.ShapeDt...]
    all_to_all x1 -> x2, starting transfers between devices: 16.7 us -> 26.9 us  [the longest x1 13.9 us: body(): main = lax.all_to_all(main, AXES, split_axis=0, concat_axis=0, tiled=True)]
    unnamed x10 -> x6, local copies, waits for them, and re-layouts: 7.97 us -> 0.01 us
  transfers between devices with their start and end apart: 2 -> 3, of which waited for: 0 -> 1; matrix products, arithmetic and copies ran while one was open for 5% -> 8% of each run, Pallas kernels for 1% -> 7%
where the time goes in v3:
time: 223 us
  waiting for transfers between devices  125 us (56%)
  Pallas kernels  28.1 us (13%)
  starting transfers between devices  27.9 us (13%)
  blocking collectives  17.4 us (8%)
  local copies, waits for them, and re-layouts  11.7 us (5%)
  other arithmetic  11.6 us (5%)
    all_to_all x1, waiting for transfers between devices, body(): main = lax.all_to_all(main, AXES, split_axis=0, concat_axis=0, tiled=True)  125 us
    all_to_all x1, blocking collectives, body(): lax.all_to_all(partial, 'y', split_axis=0, concat_axis=0, tiled=True)  17.4 us
    all_to_all x1, starting transfers between devices, body(): main = lax.all_to_all(main, AXES, split_axis=0, concat_axis=0, tiled=True)  13.9 us
    all_to_all x1, starting transfers between devices, body(): lax.all_to_all(tags, ('x', 'z', 'c'), split_axis=0, concat_axis=0, tiled=...  13 us
    pallas_call x1, Pallas kernels, gather_exchange(): pl.pallas_call(gather_kernel, grid_spec=grid_spec, out_shape=[jax.ShapeDt...  11.6 us
    pallas_call x1, Pallas kernels, make_units(): pl.pallas_call(units_kernel, in_specs=[scalars] * 3 + [pl.BlockSpec(memor...  11.5 us
    select_n x1, local copies, waits for them, and re-layouts, double_metric(): return jnp.where(same, blocks, 0).reshape(2 * NAUX, 2 * NAUX)  9.43 us
    select_n x1, other arithmetic, double_metric(): return jnp.where(same, blocks, 0).reshape(2 * NAUX, 2 * NAUX)  5.67 us
  transfers between devices with their start and end apart: 3, of which 1 were waited for; matrix products, arithmetic and copies ran while one was open for 8% of the time, Pallas kernels for 7%

profile of v3, /device:TPU:1, one launch (start us, length us, event | category | flops | bytes accessed | tf_op | source)
XLA Modules:
  0.0 222.8 jit_solution(3338566734290137667)
XLA Ops:
  0.0 0.7 fusion.16
  0.7 0.7 and_select_fusion.2
  1.4 0.2 convert_reduce_fusion.4.slot_ref
  1.6 0.1 select_reduce_fusion.2
  1.7 0.1 reshape.308
  1.8 0.7 slice_reduce_fusion.1
  2.5 0.6 concatenate.6
  3.1 0.6 broadcast_in_dim.58
  3.8 13.0 %all-to-all-start.1 = ((s32[64,1,5]{2,1,0:T(1,128)}), s32[64,1,5]{2,1,0:T(1,128)S(1)}, u32[]{:S(2)}, u32[]{:S(2)}) async-start(s32[64,1,5]{2,1,0:T(1,128)} %bitcast.7), calls=%async_computation.1 | async-start | bytes 65536 | tf_op jit(solution)/shard_map/all_to_all | solution.py:252
  16.9 0.8 fusion.spread_ref
  17.6 11.5 %units.1 = (bf16[32,8,3,32,128]{4,3,2,1,0:T(8,128)(2,1)}, bf16[32,8,1,32,128]{4,3,2,1,0:T(8,128)(2,1)}) custom-call(s32[48]{0:T(128)} %ao_ref.1, s32[48]{0:T(128)} %copy-done.1, s32[48]{0:T(128)} %copy-done.2, bf16[48,16,4096]{2,1,0:T(8,128)(2,1)} %three_ref.1, bf16[32,19968]{1,0:T(8,128)(2,1)} %coef_ref.1, bf16[2,128,512]{2,1,0:T(8,128)(2,1)} %fusion.spread_ref), custom_call_target="tpu_custom_call" | custom-call | tf_op jit(solution)/shard_map/units/pallas_call | solution.py:97
  29.1 13.9 %all-to-all-start.2 = ((bf16[256,3,32,128]{3,2,1,0:T(8,128)(2,1)}), bf16[256,3,32,128]{3,2,1,0:T(8,128)(2,1)}, u32[]{:S(2)}, u32[]{:S(2)}) async-start(bf16[256,3,32,128]{3,2,1,0:T(8,128)(2,1)} %bitcast.28), calls=%async_computation.2 | async-start | bytes 12582912 | tf_op jit(solution)/shard_map/all_to_all | solution.py:257
  43.0 0.5 broadcast_in_dim.64
  43.6 5.7 %broadcast_select_fusion = bf16[8,2,64,8,2,64]{5,4,3,2,1,0:T(2,128)(2,1)} fusion(pred[2,2]{1,0:T(4,128)(4,1)S(1)} %iota_compare_fusion.7, bf16[8,64,8,64]{3,2,1,0:T(8,128)(2,1)S(1)} %broadcast_in_dim.64), kind=kLoop, calls=%fused_computation.1 | loop fusion | flops 1048576 | bytes 2621444 | tf_op jit(solution)/shard_map/jit(_where)/select_n | solution.py:233
  49.3 9.4 %select_n.73.metric_ref = bf16[1024,1024]{1,0:T(8,128)(2,1)S(1)} reshape(bf16[8,2,64,8,2,64]{5,4,3,2,1,0:T(2,128)(2,1)} %broadcast_select_fusion) | data formatting | bytes 4194304 | tf_op jit(solution)/shard_map/jit(_where)/select_n | solution.py:233
  58.8 0.7 slice_reduce_fusion
  60.1 0.1 convert_reduce_fusion.2
  60.3 0.1 reduce_sum.96
  60.4 0.1 convert_reduce_fusion.3
  60.6 0.1 reduce_sum.91
  61.0 0.1 convert_reduce_fusion.1
  61.1 0.1 convert_reduce_fusion
  61.2 0.2 select_reduce_fusion.1
  61.4 0.2 select_reduce_fusion
  61.6 125.2 %all-to-all-done.2 = bf16[256,3,32,128]{3,2,1,0:T(8,128)(2,1)} async-done(((bf16[256,3,32,128]{3,2,1,0:T(8,128)(2,1)}), bf16[256,3,32,128]{3,2,1,0:T(8,128)(2,1)}, u32[]{:S(2)}, u32[]{:S(2)}) %all-to-all-start.2) | async-done | bytes 6291488 | tf_op jit(solution)/shard_map/all_to_all | solution.py:257
  186.7 11.6 %conditional.1 = ((bf16[2,512,1024]{2,1,0:T(8,128)(2,1)}, f32[512,512]{1,0:T(8,128)S(1)})) conditional(s32[]{:T(128)} %convert_element_type.29, (bf16[256,3,32,128]{3,2,1,0:T(8,128)(2,1)}, s32[4,48]{1,0:T(4,128)S(1)}, s32[4]{0:T(128)S(1)}, s32[1]{0:T(128)}, bf16[1024,1024]{1,0:T(8,128)(2,1)S(1)}) %tuple.13, ...), branch_computations={%region_12.13_spmd, %region_13.14_spmd} | conditional | flops 4194304 | bytes 20971528 | solution.py:272
  186.7 11.6 %gather_exchange.2 = (bf16[2,512,1024]{2,1,0:T(8,128)(2,1)}, f32[512,512]{1,0:T(8,128)S(1)}) custom-call(s32[4,48]{1,0:T(4,128)S(1)} %get-tuple-element.28.list_ref, s32[4]{0:T(128)S(1)} %get-tuple-element.29.filled_ref, s32[1]{0:T(128)} %get-tuple-element.30.core_ref, bf16[64,4,3,32,128]{4,3,2,1,0:T(8,128)(2,1)} %bitcast.in_ref, ...), custom_call_target="tpu_custom_call" | custom-call | tf_op jit(solution)/shard_map/cond/branch_0_fun/gather_exchange/pallas_call | solution.py:205
  198.3 1.1 collective-permute-start
  199.4 5.0 %own_exchange.1 = f32[512,512]{1,0:T(8,128)S(1)} custom-call(bf16[2,512,1024]{2,1,0:T(8,128)(2,1)} %get-tuple-element.53.mine_ref, bf16[1024,1024]{1,0:T(8,128)(2,1)S(1)} %select_n.73.metric_ref), custom_call_target="tpu_custom_call" | custom-call | flops 3221225472 | bytes 5242880 | tf_op jit(solution)/shard_map/own_exchange/pallas_call | solution.py:220
  204.4 0.2 add.125
  204.6 17.4 %all_to_all.27 = f32[4,128,512]{2,1,0:T(8,128)S(1)} all-to-all(f32[4,128,512]{2,1,0:T(8,128)S(1)} %bitcast.29), channel_id=1, replica_groups=mesh['x'=4,'z'=8,'c'=2,'y'=4] {'y'}, dimensions={0} | all-to-all | bytes 2097152 | tf_op jit(solution)/shard_map/all_to_all | solution.py:277
  222.0 0.8 reduce_sum.97
  (25 shorter events, 0.5 us)
Async XLA Ops:
  1.4 16.3 %copy-start.1 = (s32[48]{0:T(128)}, s32[48]{0:T(128)S(1)}, u32[]{:S(2)}) copy-start(s32[48]{0:T(128)S(1)} %get-tuple-element.83.chip_ref) | copy-start | bytes 580
  1.6 16.1 %copy-start.2 = (s32[48]{0:T(128)}, s32[48]{0:T(128)S(1)}, u32[]{:S(2)}) copy-start(s32[48]{0:T(128)S(1)} %convert_reduce_fusion.4.slot_ref) | copy-start | bytes 580
  3.8 25.3 %all-to-all-start.1 = ((s32[64,1,5]{2,1,0:T(1,128)}), s32[64,1,5]{2,1,0:T(1,128)S(1)}, u32[]{:S(2)}, u32[]{:S(2)}) async-start(s32[64,1,5]{2,1,0:T(1,128)} %bitcast.7), calls=%async_computation.1 | async-start | bytes 65536 | tf_op jit(solution)/shard_map/all_to_all | solution.py:252
  29.1 13.9 %copy-start = (bf16[512,512]{1,0:T(8,128)(2,1)S(1)}, bf16[512,512]{1,0:T(8,128)(2,1)}, u32[]{:S(2)}) copy-start(bf16[512,512]{1,0:T(8,128)(2,1)} %param.11) | copy-start | bytes 1572868
  29.1 157.6 %all-to-all-start.2 = ((bf16[256,3,32,128]{3,2,1,0:T(8,128)(2,1)}), bf16[256,3,32,128]{3,2,1,0:T(8,128)(2,1)}, u32[]{:S(2)}, u32[]{:S(2)}) async-start(bf16[256,3,32,128]{3,2,1,0:T(8,128)(2,1)} %bitcast.28), calls=%async_computation.2 | async-start | bytes 12582912 | tf_op jit(solution)/shard_map/all_to_all | solution.py:257
  198.3 6.1 %collective-permute-start = (f32[512,512]{1,0:T(8,128)S(1)}, f32[512,512]{1,0:T(8,128)S(1)}, u32[]{:S(2)}, u32[]{:S(2)}) collective-permute-start(f32[512,512]{1,0:T(8,128)S(1)} %get-tuple-element.54), channel_id=1, source_target_pairs={{0,4},{4,0},{1,5},{5,1},{2,6},{6,2},{3,7},{7,3},{8,12},{12,8},{9,1... | collective-permute-start | bytes 3145736 | tf_op jit(solution)/shard_map/ppermute | solution.py:273
